TPU v7x, 32 devices: a whole 2x2x4 slice. The times are simulated.
32 devices in a mesh: batch: 16 (over z, x, core), rank: 2 (over y).
Axes of the slice: x: 2, y: 2, z: 4, core: 2. Of those that a mesh axis runs over, the one named last changes fastest.
Arguments:
- tokens: bfloat16 [16384, 768], P('batch'), may hold values from -6 to 6
- valid_len: int32 [32], P('batch'), may hold values from 128 to 512, as said below
- w_query: bfloat16 [2, 768, 768], P(None, None, 'rank'), may hold values from -0.21875 to 0.21875
- w_key: bfloat16 [2, 768, 768], P(None, None, 'rank'), may hold values from -0.21875 to 0.21875
- w_value: bfloat16 [2, 768, 768], P(None, None, 'rank'), may hold values from -0.21875 to 0.21875
- w_out: bfloat16 [2, 768, 768], P(None, 'rank'), may hold values from -0.875 to 0.875
- w_up: bfloat16 [2, 768, 3072], P(None, None, 'rank'), may hold values from -0.21875 to 0.21875
- w_down: bfloat16 [2, 3072, 768], P(None, 'rank'), may hold values from -0.109375 to 0.109375
- mat_a: bfloat16 [768, 1024], P(None, 'rank'), may hold values from -0.21875 to 0.21875
- mat_b: bfloat16 [1024, 768], P('rank'), may hold values from -0.1875 to 0.1875
- scale_dq: float32 [2, 1024], P(None, 'rank'), may hold values from 0.25 to 2
- scale_bq: float32 [2, 768], P(None, 'rank'), may hold values from -3 to 3
- scale_dv: float32 [2, 1024], P(None, 'rank'), may hold values from 0.25 to 2
- scale_bv: float32 [2, 768], P(None, 'rank'), may hold values from -3 to 3
- cotangent: bfloat16 [16384, 768], P('batch'), may hold values from -6 to 6
Outputs:
- output: float32 [16384, 768], P('batch')
- grad_tokens: float32 [16384, 768], P('batch')
- grad_dq: float32 [2, 1024], P(None, 'rank')
- grad_bq: float32 [2, 768], P(None, 'rank')
- grad_dv: float32 [2, 1024], P(None, 'rank')
- grad_bv: float32 [2, 768], P(None, 'rank')
Inputs may be any that keep to these rules, and one draw needn't show every extreme that they name: valid_len[p] is the number of leading slots of pair p that hold tokens; at least one pair holds 512.
All inputs are finite; a program needn't handle non-finite values.
Results may differ from a plain program's by a relative error of at most 0.024.
Values may be sent and summed in bfloat16 or wider, within the bound.
A program may use at most 192 MiB of HBM per device.

v0:
```python
import jax
import jax.numpy as jnp
from jax import lax
from jax.sharding import PartitionSpec as P

HEAD_DIM = 64


epsilon = 1e-05
masked = -1e30


def normalize(values):
    center = values - jnp.mean(values, axis=-1, keepdims=True)
    spread = jnp.mean(center * center, axis=-1, keepdims=True)
    return center * lax.rsqrt(spread + epsilon)


def gelu_exact(values):
    return jax.nn.gelu(values, approximate=False)


def matmul(operand, matrix):
    return jnp.dot(operand, matrix, preferred_element_type=jnp.float32)


def matmul_back(operand, matrix):
    return jnp.einsum("td,ed->te", operand, matrix, preferred_element_type=jnp.float32)


def to_heads(rows, pair_count):
    return rows.reshape(pair_count, -1, rows.shape[1] // HEAD_DIM, HEAD_DIM)


def pair_scores(query_rows, key_rows, key_mask):
    scores = jnp.einsum(
        "qhe,khe->hqk", query_rows, key_rows, preferred_element_type=jnp.float32
    ) * HEAD_DIM ** (-0.5)
    return jnp.where(key_mask[None, None, :], scores, masked)


def attend_pair(pieces):
    query_rows, key_rows, value_rows, key_mask = pieces
    scores = pair_scores(query_rows, key_rows, key_mask)
    row_peak = jnp.max(scores, axis=-1, keepdims=True)
    exponent = jnp.exp(scores - row_peak)
    row_total = jnp.sum(exponent, axis=-1, keepdims=True)
    weights_low = (exponent / row_total).astype(jnp.bfloat16)
    mixed_rows = jnp.einsum(
        "hqk,khe->qhe", weights_low, value_rows, preferred_element_type=jnp.float32
    )
    return (mixed_rows.astype(jnp.bfloat16), row_peak[..., 0] + jnp.log(row_total[..., 0]))


def attend_back(pieces):
    query_rows, key_rows, value_rows, key_mask, log_total, incoming = pieces
    scores = pair_scores(query_rows, key_rows, key_mask)
    probs_full = jnp.exp(scores - log_total[..., None])
    dprob = jnp.einsum("qhe,khe->hqk", incoming, value_rows, preferred_element_type=jnp.float32)
    grad_value = jnp.einsum(
        "hqk,qhe->khe",
        probs_full.astype(jnp.bfloat16),
        incoming,
        preferred_element_type=jnp.float32,
    )
    row_delta = jnp.sum(probs_full * dprob, axis=-1, keepdims=True)
    dscore = (probs_full * (dprob - row_delta)).astype(jnp.bfloat16)
    grad_query = jnp.einsum(
        "hqk,khe->qhe", dscore, key_rows, preferred_element_type=jnp.float32
    ) * HEAD_DIM ** (-0.5)
    grad_key = jnp.einsum(
        "hqk,qhe->khe", dscore, query_rows, preferred_element_type=jnp.float32
    ) * HEAD_DIM ** (-0.5)
    return (
        grad_query.astype(jnp.bfloat16),
        grad_key.astype(jnp.bfloat16),
        grad_value.astype(jnp.bfloat16),
    )


def layer_forward(inputs, key_mask, weights, shared_a, shared_b):
    w_query, w_key, w_value, w_out, w_up, w_down, scale_dq, scale_bq, scale_dv, scale_bv = weights
    pair_count = key_mask.shape[0]
    rows_low = inputs.astype(jnp.bfloat16)
    inner = matmul(rows_low, shared_a)
    part_query = matmul((inner * scale_dq).astype(jnp.bfloat16), shared_b)
    part_value = matmul((inner * scale_dv).astype(jnp.bfloat16), shared_b)
    lift_query, lift_value = (
        lax.psum_scatter(part_query, "rank", scatter_dimension=1, tiled=True),
        lax.psum_scatter(part_value, "rank", scatter_dimension=1, tiled=True),
    )
    query_rows = (matmul(rows_low, w_query) + lift_query * scale_bq).astype(jnp.bfloat16)
    key_rows = matmul(rows_low, w_key).astype(jnp.bfloat16)
    value_rows = (matmul(rows_low, w_value) + lift_value * scale_bv).astype(jnp.bfloat16)
    mixed_rows, log_total = lax.map(
        attend_pair,
        (
            to_heads(query_rows, pair_count),
            to_heads(key_rows, pair_count),
            to_heads(value_rows, pair_count),
            key_mask,
        ),
    )
    attended = mixed_rows.reshape(inputs.shape[0], -1)
    out_part = matmul(attended, w_out)
    out_sum = lax.psum(out_part, "rank")
    first_sum = inputs + out_sum
    normed = normalize(first_sum)
    before = matmul(normed.astype(jnp.bfloat16), w_up)
    hidden = gelu_exact(before).astype(jnp.bfloat16)
    ffn_part = matmul(hidden, w_down)
    ffn_sum = lax.psum(ffn_part, "rank")
    second_sum = normed + ffn_sum
    saved = (
        inner,
        lift_query,
        lift_value,
        query_rows,
        key_rows,
        value_rows,
        log_total,
        first_sum,
        before,
        second_sum,
    )
    return (normalize(second_sum), saved)


def layer_backward(inputs, key_mask, weights, shared_a, shared_b, upstream):
    w_query, w_key, w_value, w_out, w_up, w_down, scale_dq, scale_bq, scale_dv, scale_bv = weights
    pair_count = key_mask.shape[0]
    unused, saved = layer_forward(inputs, key_mask, weights, shared_a, shared_b)
    (
        inner,
        lift_query,
        lift_value,
        query_rows,
        key_rows,
        value_rows,
        log_total,
        first_sum,
        before,
        second_sum,
    ) = saved
    unused, second_back = jax.vjp(normalize, second_sum)
    grad_second = second_back(upstream)[0]
    grad_hidden = matmul_back(grad_second.astype(jnp.bfloat16), w_down)
    unused, gelu_back = jax.vjp(gelu_exact, before)
    grad_before = gelu_back(grad_hidden)[0].astype(jnp.bfloat16)
    back_part = matmul_back(grad_before, w_up)
    back_sum = lax.psum(back_part, "rank")
    unused, first_back = jax.vjp(normalize, first_sum)
    grad_first = first_back(grad_second + back_sum)[0]
    grad_attended = matmul_back(grad_first.astype(jnp.bfloat16), w_out).astype(jnp.bfloat16)
    grad_query, grad_key, grad_value = lax.map(
        attend_back,
        (
            to_heads(query_rows, pair_count),
            to_heads(key_rows, pair_count),
            to_heads(value_rows, pair_count),
            key_mask,
            log_total,
            to_heads(grad_attended, pair_count),
        ),
    )
    row_count = inputs.shape[0]
    grad_query = grad_query.reshape(row_count, -1)
    grad_key = grad_key.reshape(row_count, -1)
    grad_value = grad_value.reshape(row_count, -1)
    grad_bq = jnp.sum(grad_query.astype(jnp.float32) * lift_query, axis=0)
    grad_bv = jnp.sum(grad_value.astype(jnp.float32) * lift_value, axis=0)
    pass_query = (grad_query * scale_bq).astype(jnp.bfloat16)
    pass_value = (grad_value * scale_bv).astype(jnp.bfloat16)
    full_query, full_value = (
        lax.all_gather(pass_query, "rank", axis=1, tiled=True),
        lax.all_gather(pass_value, "rank", axis=1, tiled=True),
    )
    rank_query = matmul_back(full_query, shared_b)
    rank_value = matmul_back(full_value, shared_b)
    grad_dq = jnp.sum(rank_query * inner, axis=0)
    grad_dv = jnp.sum(rank_value * inner, axis=0)
    grad_inner = (rank_query * scale_dq + rank_value * scale_dv).astype(jnp.bfloat16)
    input_part = (
        matmul_back(grad_query, w_query)
        + matmul_back(grad_key, w_key)
        + matmul_back(grad_value, w_value)
        + matmul_back(grad_inner, shared_a)
    )
    input_sum = lax.psum(input_part, "rank")
    return (grad_first + input_sum, (grad_dq, grad_bq, grad_dv, grad_bv))


def on_device(
    tokens,
    valid_len,
    w_query,
    w_key,
    w_value,
    w_out,
    w_up,
    w_down,
    mat_a,
    mat_b,
    scale_dq,
    scale_bq,
    scale_dv,
    scale_bv,
    cotangent,
):
    stacked = (w_query, w_key, w_value, w_out, w_up, w_down)
    vectors = (scale_dq, scale_bq, scale_dv, scale_bv)
    seq_len = tokens.shape[0] // valid_len.shape[0]
    key_mask = jnp.arange(seq_len, dtype=jnp.int32)[None, :] < valid_len[:, None]
    level_count = stacked[0].shape[0]
    layer_inputs = []
    level_weights = []
    current = tokens.astype(jnp.float32)
    for level_index in range(level_count):
        weights = tuple((stacked_array[level_index] for stacked_array in stacked)) + tuple(
            (vector_array[level_index] for vector_array in vectors)
        )
        level_weights.append(weights)
        layer_inputs.append(current)
        current, unused = layer_forward(current, key_mask, weights, mat_a, mat_b)
    upstream = cotangent.astype(jnp.float32)
    collected = [None] * level_count
    for level_index in reversed(range(level_count)):
        upstream, collected[level_index] = layer_backward(
            layer_inputs[level_index], key_mask, level_weights[level_index], mat_a, mat_b, upstream
        )
    totals = tuple(
        (
            jnp.stack([level_grads[member_index] for level_grads in collected])
            for member_index in range(4)
        )
    )
    totals = lax.psum(totals, "batch")
    return (current, upstream, totals[0], totals[1], totals[2], totals[3])


def solution(mesh):
    return jax.shard_map(
        on_device,
        mesh=mesh,
        in_specs=(
            P("batch", None),
            P("batch"),
            P(None, None, "rank"),
            P(None, None, "rank"),
            P(None, None, "rank"),
            P(None, "rank", None),
            P(None, None, "rank"),
            P(None, "rank", None),
            P(None, "rank"),
            P("rank", None),
            P(None, "rank"),
            P(None, "rank"),
            P(None, "rank"),
            P(None, "rank"),
            P("batch", None),
        ),
        out_specs=(
            P("batch", None),
            P("batch", None),
            P(None, "rank"),
            P(None, "rank"),
            P(None, "rank"),
            P(None, "rank"),
        ),
        check_vma=False,
    )
```

profile of v0, /device:TPU:0, one launch (start us, length us, event | category | flops | bytes accessed | tf_op | source)
XLA Modules:
  0.0 1581.5 jit_solution(18011608223874051577)
XLA Ops:
  15.2 4.4 fusion.323
  19.8 2.9 convolution_convert_fusion.1
  27.4 33.4 %reduce-scatter.5.cloned.1.call-done = f32[1024,384]{1,0:T(8,128)} async-done(((f32[1024,768]{1,0:T(8,128)}), f32[1024,384]{1,0:T(8,128)}) %reduce-scatter.5.cloned.1.call-update) | async-done | bytes 1572880 | tf_op jit(solution)/shard_map/reduce_scatter | solution.py:90
  60.8 3.5 add_convert_fusion.19
  66.5 3.2 reshape.281
  72.1 35.0 %reduce-scatter.7.cloned.1.call-done = f32[1024,384]{1,0:T(8,128)} async-done(((f32[1024,768]{1,0:T(8,128)}), f32[1024,384]{1,0:T(8,128)}) %reduce-scatter.7.cloned.1.call-update) | async-done | bytes 1572880 | tf_op jit(solution)/shard_map/reduce_scatter | solution.py:89
  107.1 3.5 add_convert_fusion.18
  115.7 18.5 %while.72 = (s32[]{:T(128)}, bf16[2,512,6,64]{1,3,2,0:T(8,128)(2,1)}, bf16[2,512,6,64]{1,3,2,0:T(8,128)(2,1)S(1)}, pred[2,512]{1,0:T(4,128)(4,1)S(1)}, bf16[2,51...) while((s32[]{:T(128)}, bf16[2,512,6,64]{1,3,2,0:T(8,128)(2,1)}, ...), condition=%wide.region_5.6_spmd, body=%wide.region_2.5_spmd.sunk | while | flops 412287488 | bytes 14188113 | solution.py:95
  115.7 5.0 fusion.573
  120.7 4.2 fusion.574
  124.9 5.0 fusion.573
  130.0 4.2 fusion.574
  139.8 85.6 %all-reduce.14.cloned.1.call-done = f32[1024,768]{1,0:T(8,128)} async-done(((f32[1024,768]{1,0:T(8,128)}), f32[1024,768]{1,0:T(8,128)}) %all-reduce.14.cloned.1.call-update) | async-done | bytes 3145744 | tf_op jit(solution)/shard_map/psum | solution.py:106
  229.1 22.1 %fusion.235 = f32[1024,768]{1,0:T(8,128)} fusion(bf16[2,1536,768]{2,1,0:T(8,128)(2,1)} %param.34, bf16[2,768,1536]{2,1,0:T(8,128)(2,1)} %param.33, f32[1024]{0:T(1024)S(1)} %add_rsqrt_fusion.3, f32[1024]{0:T(1024)S(1)} %broadcast_multiply_fusion.7, f32[1024,768]{1,0:T(8,128)} %all-reduce.14.cloned.1.call-done, bf16[1024,768]{1,0:T(8,128)(2,1)S(1)} %copy-done.17), kind=kOutput, calls=%fused_computation.287 | convolution fusion | flops 4938006528 | bytes 12591104 | tf_op jit(solution)/shard_map/dot_general | solution.py:24
  251.3 85.9 %all-reduce.16.cloned.1.call-done = f32[1024,768]{1,0:T(8,128)} async-done(((f32[1024,768]{1,0:T(8,128)}), f32[1024,768]{1,0:T(8,128)}) %all-reduce.16.cloned.1.call-update) | async-done | bytes 3145744 | tf_op jit(solution)/shard_map/psum | solution.py:112
  337.2 3.7 fusion.465
  358.2 32.3 %reduce-scatter.11.cloned.1.call-done = f32[1024,384]{1,0:T(8,128)} async-done(((f32[1024,768]{1,0:T(8,128)}), f32[1024,384]{1,0:T(8,128)}) %reduce-scatter.11.cloned.1.call-update) | async-done | bytes 1572880 | tf_op jit(solution)/shard_map/reduce_scatter | solution.py:89
  390.5 3.5 add_convert_fusion.16
  398.1 38.5 %reduce-scatter.9.cloned.1.call-done = f32[1024,384]{1,0:T(8,128)} async-done(((f32[1024,768]{1,0:T(8,128)}), f32[1024,384]{1,0:T(8,128)}) %reduce-scatter.9.cloned.1.call-update) | async-done | bytes 1572880 | tf_op jit(solution)/shard_map/reduce_scatter | solution.py:90
  436.6 3.7 add_convert_fusion.17
  445.4 11.0 while.74
  462.4 85.5 %all-reduce.18.cloned.1.call-done = f32[1024,768]{1,0:T(8,128)} async-done(((f32[1024,768]{1,0:T(8,128)}), f32[1024,768]{1,0:T(8,128)}) %all-reduce.18.cloned.1.call-update) | async-done | bytes 3145744 | tf_op jit(solution)/shard_map/psum | solution.py:106
  547.9 3.7 fusion.463
  553.0 16.5 %fusion.202 = (f32[1024,1536]{1,0:T(8,128)S(1)}, f32[1024,1536]{1,0:T(8,128)S(1)}) fusion(bf16[2,768,1536]{2,1,0:T(8,128)(2,1)} %param.33, f32[1024,768]{1,0:T(8,128)S(1)} %get-tuple-element.493, f32[1024]{0:T(1024)S(1)} %fusion.381, f32[1024]{0:T(1024)S(1)} %broadcast_multiply_fusion.3), kind=kOutput, calls=%fused_computation.198 | convolution fusion | flops 2515795968 | bytes 18096128 | tf_op jit(solution)/shard_map/dot_general | solution.py:24
  574.1 4.3 fusion.229
  580.0 14.2 while.76
  583.6 3.6 fusion.599
  590.8 3.5 fusion.599
  599.2 65.2 %all-reduce.20.cloned.1.call-done = f32[1024,768]{1,0:T(8,128)} async-done(((f32[1024,768]{1,0:T(8,128)}), f32[1024,768]{1,0:T(8,128)}) %all-reduce.20.cloned.1.call-update) | async-done | bytes 3145744 | tf_op jit(solution)/shard_map/psum | solution.py:112
  664.3 3.5 fusion.462
  671.8 14.0 fusion.237
  685.8 153.6 %all-reduce.28.cloned.1.call-done = (f32[1024,768]{1,0:T(8,128)}, f32[1024,768]{1,0:T(8,128)}) async-done(((f32[1024,768]{1,0:T(8,128)}, f32[1024,768]{1,0:T(8,128)}), (f32[1024,768]{1,0:T(8,128)}, f32[1024,768]{1,0:T(8,128)})) %all-reduce.28.cloned.1.call-update) | async-done | bytes 6291472 | tf_op jit(solution)/shard_map/psum | solution.py:106
  839.5 7.5 fusion.460
  853.6 3.4 reshape.290
  862.0 21.1 %while.75 = (s32[]{:T(128)}, bf16[2,512,6,64]{1,3,2,0:T(8,128)(2,1)}, bf16[2,512,6,64]{1,3,2,0:T(8,128)(2,1)}, bf16[2,512,6,64]{1,3,2,0:T(8,128)(2,1)}, bf16[2,5...) while((s32[]{:T(128)}, ...), condition=%wide.region_41.42_spmd, body=%wide.region_39.41_spmd.sunk | while | flops 1031205888 | bytes 66948864 | solution.py:155
  888.4 3.3 fusion.293
  894.6 19.5 %fusion.203 = (f32[1024,1536]{1,0:T(8,128)}, f32[1024,1536]{1,0:T(8,128)}) fusion(bf16[2,768,1536]{2,1,0:T(8,128)(2,1)} %param.33, f32[1024,768]{1,0:T(8,128)S(1)} %copy-done.2, f32[1024]{0:T(1024)S(1)} %fusion.383, f32[1024]{0:T(1024)S(1)} %broadcast_multiply_fusion.1), kind=kOutput, calls=%fused_computation.199 | convolution fusion | flops 2515795968 | bytes 18096128 | tf_op jit(solution)/shard_map/dot_general | solution.py:24
  930.2 4.1 fusion.339
  934.2 10.4 fusion.230
  944.6 3.7 fusion.488
  948.4 8.7 all-gather.7.cloned.1.call-done
  957.1 4.5 multiply_reduce_fusion.13
  962.3 5.2 add_add_fusion.5
  968.5 19.2 %while.73 = (s32[]{:T(128)}, bf16[2,512,6,64]{1,3,2,0:T(8,128)(2,1)}, bf16[2,512,6,64]{1,3,2,0:T(8,128)(2,1)S(1)}, pred[2,512]{1,0:T(4,128)(4,1)S(1)}, bf16[2,51...) while((s32[]{:T(128)}, bf16[2,512,6,64]{1,3,2,0:T(8,128)(2,1)}, ...), condition=%wide.region_17.18_spmd, body=%wide.region_14.17_spmd.sunk | while | flops 412287488 | bytes 14188113 | solution.py:95
  968.6 5.4 fusion.578
  973.9 4.3 fusion.579
  978.3 5.0 fusion.578
  983.2 4.5 fusion.579
  992.6 128.6 %all-reduce.26.cloned.1.call-done = (f32[1024,768]{1,0:T(8,128)}, f32[1024,768]{1,0:T(8,128)}) async-done(((f32[1024,768]{1,0:T(8,128)}, f32[1024,768]{1,0:T(8,128)}), (f32[1024,768]{1,0:T(8,128)}, f32[1024,768]{1,0:T(8,128)})) %all-reduce.26.cloned.1.call-update) | async-done | bytes 6291472 | tf_op jit(solution)/shard_map/psum | solution.py:112
  1121.2 3.7 fusion.458
  1130.0 14.0 fusion.238
  1144.2 153.5 %all-reduce.24.cloned.1.call-done = (f32[1024,768]{1,0:T(8,128)}, f32[1024,768]{1,0:T(8,128)}) async-done(((f32[1024,768]{1,0:T(8,128)}, f32[1024,768]{1,0:T(8,128)}), (f32[1024,768]{1,0:T(8,128)}, f32[1024,768]{1,0:T(8,128)})) %all-reduce.24.cloned.1.call-update) | async-done | bytes 6291472 | tf_op jit(solution)/shard_map/psum | solution.py:106
  1297.7 4.7 multiply_reduce_fusion.2
  1309.8 3.4 reshape.295
  1318.2 22.4 %while.77 = (s32[]{:T(128)}, bf16[2,512,6,64]{1,3,2,0:T(8,128)(2,1)}, bf16[2,512,6,64]{1,3,2,0:T(8,128)(2,1)}, bf16[2,512,6,64]{1,3,2,0:T(8,128)(2,1)}, bf16[2,5...) while((s32[]{:T(128)}, ...), condition=%wide.region_60.61_spmd, body=%wide.region_58.60_spmd.sunk | while | flops 1031205888 | bytes 66948864 | solution.py:155
  1349.2 3.5 fusion.455
  1356.7 21.9 %fusion.233 = f32[1024,768]{1,0:T(8,128)} fusion(bf16[2,1536,768]{2,1,0:T(8,128)(2,1)} %param.34, bf16[2,768,1536]{2,1,0:T(8,128)(2,1)} %param.33, f32[1024,768]{1,0:T(8,128)} %copy-done.19, f32[1024]{0:T(1024)S(1)} %add_rsqrt_fusion.1, f32[1024]{0:T(1024)S(1)} %broadcast_multiply_fusion.5), kind=kOutput, calls=%fused_computation.286 | convolution fusion | flops 4936433664 | bytes 11018240 | tf_op jit(solution)/shard_map/dot_general | solution.py:24
  1387.9 3.9 fusion.489
  1391.9 10.5 all-gather.11.cloned.1.call-done
  1402.4 3.2 multiply_reduce_fusion.14
  1407.0 5.2 add_add_fusion.4
  1413.0 61.2 %all-reduce = (f32[2,512]{1,0:T(2,128)}, f32[2,384]{1,0:T(2,128)}, f32[2,512]{1,0:T(2,128)}, f32[2,384]{1,0:T(2,128)}) all-reduce(f32[2,512]{1,0:T(2,128)S(1)} %pad_maximum_fusion, f32[2,384]{1,0:T(2,128)S(1)} %pad_maximum_fusion.2, f32[2,512]{1,0:T(2,128)S(1)} %pad_maximum_fusion.1, ...), channel_id=1, replica_groups=mesh['batch'=16,'rank'=2] {'batch'}, use_global_device_ids=true, to_apply=%region_64.65 | all-reduce | flops 3584 | bytes 28672 | tf_op jit(solution)/shard_map/psum | solution.py:237
  1474.2 91.8 %all-reduce.22.cloned.1.call-done = (f32[1024,768]{1,0:T(8,128)}, f32[1024,768]{1,0:T(8,128)}) async-done(((f32[1024,768]{1,0:T(8,128)}, f32[1024,768]{1,0:T(8,128)}), (f32[1024,768]{1,0:T(8,128)}, f32[1024,768]{1,0:T(8,128)})) %all-reduce.22.cloned.1.call-update) | async-done | bytes 6291472 | tf_op jit(solution)/shard_map/psum | solution.py:112
  1565.9 5.0 add_add_fusion.6
  (469 shorter events, 229.3 us)
Async XLA Ops:
  7.2 53.6 %reduce-scatter.5.cloned.1.call-start = ((), (), s32[]{:S(2)}) async-start(), calls=%async_computation.4 | async-start | bytes 4718592 | tf_op jit(solution)/shard_map/reduce_scatter | solution.py:90
  8.0 339.0 %copy-start.101 = (f32[1,512]{1,0:T(1,128)}, f32[1,512]{1,0:T(1,128)S(1)}, u32[]{:S(2)}) copy-start(f32[1,512]{1,0:T(1,128)S(1)} %get-tuple-element.522) | copy-start | bytes 6148
  14.6 92.5 %reduce-scatter.7.cloned.1.call-start = ((), (), s32[]{:S(2)}) async-start(), calls=%async_computation.5 | async-start | bytes 4718592 | tf_op jit(solution)/shard_map/reduce_scatter | solution.py:89
  14.7 329.6 %copy-start.103 = (f32[1,512]{1,0:T(1,128)}, f32[1,512]{1,0:T(1,128)S(1)}, u32[]{:S(2)}) copy-start(f32[1,512]{1,0:T(1,128)S(1)} %get-tuple-element.520) | copy-start | bytes 6148
  19.6 205.9 %all-reduce.14.cloned.1.call-start = ((), (), s32[]{:S(2)}) async-start(), calls=%async_computation.6 | async-start | bytes 6291456 | tf_op jit(solution)/shard_map/psum | solution.py:106
  27.2 42.5 %copy-start.89 = (f32[384]{0:T(512)}, f32[384]{0:T(512)S(1)}, u32[]{:S(2)}) copy-start(f32[384]{0:T(512)S(1)} %get-tuple-element.369) | copy-start | bytes 4612
  27.2 409.4 %copy-start.93 = (f32[384]{0:T(512)}, f32[384]{0:T(512)S(1)}, u32[]{:S(2)}) copy-start(f32[384]{0:T(512)S(1)} %get-tuple-element.368) | copy-start | bytes 4612
  27.3 79.8 %copy-start.91 = (f32[384]{0:T(512)}, f32[384]{0:T(512)S(1)}, u32[]{:S(2)}) copy-start(f32[384]{0:T(512)S(1)} %get-tuple-element.367) | copy-start | bytes 4612
  27.3 363.2 %copy-start.95 = (f32[384]{0:T(512)}, f32[384]{0:T(512)S(1)}, u32[]{:S(2)}) copy-start(f32[384]{0:T(512)S(1)} %get-tuple-element.366) | copy-start | bytes 4612
  110.5 5.1 copy-start.41
  134.2 5.4 copy-start.6
  134.2 5.4 copy-start.9
  139.6 85.9 %copy-start.17 = (bf16[1024,768]{1,0:T(8,128)(2,1)S(1)}, bf16[1024,768]{1,0:T(8,128)(2,1)}, u32[]{:S(2)}) copy-start(bf16[1024,768]{1,0:T(8,128)(2,1)} %param.27) | copy-start | bytes 4718596
  139.6 197.6 %all-reduce.16.cloned.1.call-start = ((), (), s32[]{:S(2)}) async-start(), calls=%async_computation.7 | async-start | bytes 6291456 | tf_op jit(solution)/shard_map/psum | solution.py:112
  251.2 139.2 %reduce-scatter.11.cloned.1.call-start = ((), (), s32[]{:S(2)}) async-start(), calls=%async_computation.9 | async-start | bytes 4718592 | tf_op jit(solution)/shard_map/reduce_scatter | solution.py:89
  340.9 207.0 %copy-start.79 = (f32[1024]{0:T(1024)}, f32[1024]{0:T(1024)S(1)}, u32[]{:S(2)}) copy-start(f32[1024]{0:T(1024)S(1)} %broadcast_multiply_fusion.6) | copy-start | bytes 12292
  341.5 206.4 %copy-start.81 = (f32[1024]{0:T(1024)}, f32[1024]{0:T(1024)S(1)}, u32[]{:S(2)}) copy-start(f32[1024]{0:T(1024)S(1)} %add_rsqrt_fusion.2) | copy-start | bytes 12292
  347.0 89.6 %reduce-scatter.9.cloned.1.call-start = ((), (), s32[]{:S(2)}) async-start(), calls=%async_computation.8 | async-start | bytes 4718592 | tf_op jit(solution)/shard_map/reduce_scatter | solution.py:90
  349.7 198.1 %all-reduce.18.cloned.1.call-start = ((), (), s32[]{:S(2)}) async-start(), calls=%async_computation.10 | async-start | bytes 6291456 | tf_op jit(solution)/shard_map/psum | solution.py:106
  393.9 42.7 %copy-start.61 = (bf16[2,768,384]{2,1,0:T(8,128)(2,1)S(1)}, bf16[2,768,384]{2,1,0:T(8,128)(2,1)}, u32[]{:S(2)}) copy-start(bf16[2,768,384]{2,1,0:T(8,128)(2,1)} %param.31) | copy-start | bytes 3538948
  456.4 5.5 copy-start.12
  456.4 5.5 copy-start.14
  456.4 5.5 copy-start.43
  456.4 5.5 copy-start.77
  461.9 202.4 %all-reduce.20.cloned.1.call-start = ((), (), s32[]{:S(2)}) async-start(), calls=%async_computation.11 | async-start | bytes 6291456 | tf_op jit(solution)/shard_map/psum | solution.py:112
  547.9 26.2 %slice-start = ((s8[4718592]{0:T(1024)(128)(4,1)}), s8[4194304]{0:T(1024)(128)(4,1)S(1)}, s32[]{:S(2)}) async-start(s8[4718592]{0:T(1024)(128)(4,1)} %bitcast.492), calls=%async_computation.20 | async-start | bytes 8388608
  551.5 18.0 %copy-start.4 = (f32[1024,768]{1,0:T(8,128)}, f32[1024,768]{1,0:T(8,128)S(1)}, u32[]{:S(2)}) copy-start(f32[1024,768]{1,0:T(8,128)S(1)} %get-tuple-element.493) | copy-start | bytes 9437188
  553.0 21.1 %slice-start.1 = ((s8[4718592]{0:T(1024)(128)(4,1)}), s8[524288]{0:T(1024)(128)(4,1)S(1)}, s32[]{:S(2)}) async-start(s8[4718592]{0:T(1024)(128)(4,1)} %bitcast.492), calls=%async_computation.21 | async-start | bytes 1048576
  578.4 261.1 %all-reduce.28.cloned.1.call-start = ((), (), s32[]{:S(2)}) async-start(), calls=%async_computation.19 | async-start | bytes 12582912 | tf_op jit(solution)/shard_map/psum | solution.py:106
  599.2 68.7 %copy-start.54 = (bf16[1024,768]{1,0:T(8,128)(2,1)S(1)}, bf16[1024,768]{1,0:T(8,128)(2,1)}, u32[]{:S(2)}) copy-start(bf16[1024,768]{1,0:T(8,128)(2,1)} %param.41) | copy-start | bytes 4718596
  685.8 153.7 %copy-start.18 = (bf16[1024,768]{1,0:T(8,128)(2,1)S(1)}, bf16[1024,768]{1,0:T(8,128)(2,1)}, u32[]{:S(2)}) copy-start(bf16[1024,768]{1,0:T(8,128)(2,1)} %param.27) | copy-start | bytes 4718596
  685.8 258.8 %all-gather.5.cloned.1.call-start = ((), (), s32[]{:S(2)}) async-start(), calls=%async_computation.12 | async-start | bytes 2359296 | tf_op jit(solution)/shard_map/all_gather | solution.py:175
  839.5 7.5 copy-start.88
  839.5 7.6 copy-start.5
  839.5 7.7 copy-start.21
  839.5 8.6 copy-start.37
  853.6 8.4 copy-start.13
  853.6 8.4 copy-start.15
  853.6 8.4 copy-start.44
  853.6 8.4 copy-start.78
  883.1 5.3 copy-start.96
  886.1 5.7 copy-start.105
  891.8 65.3 %all-gather.7.cloned.1.call-start = ((), (), s32[]{:S(2)}) async-start(), calls=%async_computation.13 | async-start | bytes 2359296 | tf_op jit(solution)/shard_map/all_gather | solution.py:176
  894.4 19.8 %copy-start.85 = (f32[1024]{0:T(1024)}, f32[1024]{0:T(1024)S(1)}, u32[]{:S(2)}) copy-start(f32[1024]{0:T(1024)S(1)} %multiply_reduce_fusion.5) | copy-start | bytes 12292
  916.1 6.5 copy-start.94
  929.7 191.5 %all-reduce.26.cloned.1.call-start = ((), (), s32[]{:S(2)}) async-start(), calls=%async_computation.18 | async-start | bytes 12582912 | tf_op jit(solution)/shard_map/psum | solution.py:112
  948.4 13.2 copy-start.102
  948.4 13.2 copy-start.104
  957.1 5.2 copy-start.47
  967.5 330.2 %all-reduce.24.cloned.1.call-start = ((), (), s32[]{:S(2)}) async-start(), calls=%async_computation.17 | async-start | bytes 12582912 | tf_op jit(solution)/shard_map/psum | solution.py:106
  1144.0 243.9 %all-gather.9.cloned.1.call-start = ((), (), s32[]{:S(2)}) async-start(), calls=%async_computation.14 | async-start | bytes 2359296 | tf_op jit(solution)/shard_map/all_gather | solution.py:175
  1297.7 5.6 copy-start.22
  1297.7 6.5 copy-start.38
  1309.8 8.4 copy-start.8
  1309.8 8.4 copy-start.11
  1309.8 8.4 copy-start.42
  1346.3 56.1 %all-gather.11.cloned.1.call-start = ((), (), s32[]{:S(2)}) async-start(), calls=%async_computation.15 | async-start | bytes 2359296 | tf_op jit(solution)/shard_map/all_gather | solution.py:176
  1356.6 21.9 %copy-start.70 = (bf16[2,512,6,64]{1,3,2,0:T(8,128)(2,1)S(1)}, bf16[2,512,6,64]{1,3,2,0:T(8,128)(2,1)}, u32[]{:S(2)}) copy-start(bf16[2,512,6,64]{1,3,2,0:T(8,128)(2,1)} %get-tuple-element.264) | copy-start | bytes 2359300
  1356.6 209.3 %all-reduce.22.cloned.1.call-start = ((), (), s32[]{:S(2)}) async-start(), calls=%async_computation.16 | async-start | bytes 12582912 | tf_op jit(solution)/shard_map/psum | solution.py:112
  1387.9 14.5 copy-start.29
  1391.9 13.8 copy-start.98
  1391.9 13.8 copy-start.100
  1565.9 5.0 copy-start.20
  1565.9 5.5 copy-start.65
  (78 other events, 200.7 us)
Sparse Core Ops, SparseCore 0:
  14.7 46.0 reduce-scatter.4
  63.7 43.3 reduce-scatter.6
  139.7 85.7 all-reduce.13
  251.4 85.7 all-reduce.15
  347.1 43.3 reduce-scatter.10
  393.2 43.3 reduce-scatter.8
  462.0 85.7 all-reduce.17
  578.5 85.7 all-reduce.19
  685.9 153.5 all-reduce.27
  891.9 27.2 all-gather.4
  929.8 27.2 all-gather.6
  967.6 153.5 all-reduce.25
  1144.1 153.5 all-reduce.23
  1346.4 27.2 all-gather.8
  1375.2 27.1 all-gather.10
  1412.3 153.5 all-reduce.21
where the time goes:
time: 1590 us; the launch traced here: 1580 us
  waiting for transfers between devices  1010 us (64%)
  matrix products  300 us (19%)
  local copies, waits for them, and re-layouts  112 us (7%)
  other arithmetic  81.6 us (5%)
  blocking collectives  61.2 us (4%)
    psum x4, waiting for transfers between devices, layer_forward(): out_sum = lax.psum(out_part, 'rank')  478 us
    psum x4, waiting for transfers between devices, layer_forward(): ffn_sum = lax.psum(ffn_part, 'rank')  371 us
    dot_general x22, matrix products, matmul(): return jnp.dot(operand, matrix, preferred_element_type=jnp.float32)  141 us
    dot_general x16, matrix products, matmul_back(): jnp.einsum('td,ed->te', operand, matrix, preferred_element_type=jnp.float32)  73.3 us
    reduce_scatter x2, waiting for transfers between devices, layer_forward(): lax.psum_scatter(part_value, 'rank', scatter_dimension=1, tiled=True)  71.9 us
    reduce_scatter x2, waiting for transfers between devices, layer_forward(): lax.psum_scatter(part_query, 'rank', scatter_dimension=1, tiled=True)  67.2 us
    psum x1, blocking collectives, on_device(): totals = lax.psum(totals, 'batch')  61.2 us
    reduce_sum x12, other arithmetic, normalize(): center = values - jnp.mean(values, axis=-1, keepdims=True)  37.6 us
  transfers between devices with their start and end apart: 16, of which 14 were waited for; matrix products, arithmetic and copies ran while one was open for 12% of the time, Pallas kernels for 0%

commit v1 on v0

v1 whole, which is shorter than its diff:
```python
import functools

import jax
import jax.numpy as jnp
from jax import lax
from jax.experimental import pallas as pl
from jax.experimental.pallas import tpu as pltpu
from jax.sharding import PartitionSpec as P

HEAD_DIM = 64
MESH = pl.DeviceIdType.MESH

epsilon = 1e-05
masked = -1e30


def flip(index, bit):
    step = 1 << bit
    return index + step - 2 * step * ((index // step) % 2)


class Exchange:
    LAG = 4
    HOP = 2

    def __init__(self, groups, loads, sems):
        self.groups, self.loads = groups, loads
        self.y_send, self.y_recv, self.x_send, self.x_recv, self.z_send, self.z_recv, self.c_send, self.c_recv = sems
        self.batch = lax.axis_index("batch")
        self.rank = lax.axis_index("rank")
        b = self.batch
        self.core = b % 2
        bit_x, bit_z = (b // 2) % 2, (b // 4) % 2
        self.partner = {
            "y": (b, 1 - self.rank),
            "x": (flip(b, 1), self.rank),
            "z": (flip(b, 2), self.rank),
            "c": (flip(b, 0), self.rank),
        }
        chip = lambda cx, cz: cx + 2 * cz
        own, across, along, far = (
            chip(bit_x, bit_z),
            chip(1 - bit_x, bit_z),
            chip(bit_x, 1 - bit_z),
            chip(1 - bit_x, 1 - bit_z),
        )
        parity = (bit_x + bit_z) % 2
        first = lambda who: 2 * who
        second = lambda who: 2 * who + 1
        pair = lambda par, which: 8 + 2 * par + which
        self.y_units = [first(own), second(own), pair(parity, 0), pair(parity, 1)]
        self.x_units = [first(across), second(across), pair(1 - parity, 0), second(far)]
        self.z_units = [first(along), second(along), first(far), pair(1 - parity, 1)]
        self.x_out = [first(own), second(own), pair(parity, 0), second(along)]
        self.z_out = [first(own), second(own), first(across), pair(parity, 1)]
        self.count = 4 * len(groups)
        self.pending = []
        self.next_tick = 0
        self.plan()

    def barrier(self):
        bar = pltpu.get_barrier_semaphore()
        for who in self.partner.values():
            pl.semaphore_signal(bar, inc=1, device_id=who, device_id_type=MESH)
        pl.semaphore_wait(bar, len(self.partner))

    def copy(self, src, dst, send, recv, link):
        return pltpu.make_async_remote_copy(
            src_ref=src, dst_ref=dst, send_sem=send, recv_sem=recv,
            device_id=self.partner[link], device_id_type=MESH,
        )

    def full(self, group, unit, core, rank):
        return self.groups[group](2 * unit + core, rank)

    def y_copy(self, item):
        g, j = divmod(item, 4)
        ref = self.full(g, self.y_units[j], self.core, self.rank)
        return self.copy(ref, ref, self.y_send.at[item], self.y_recv.at[item], "y")

    def plane_copy(self, item, link):
        g, j = divmod(item, 4)
        unit = (self.x_out if link == "x" else self.z_out)[j]
        send, recv = (self.x_send, self.x_recv) if link == "x" else (self.z_send, self.z_recv)
        ref = self.full(g, unit, self.core, 1 - self.rank)
        return self.copy(ref, ref, send.at[item], recv.at[item], link)

    def core_copy(self, item, link):
        g, j = divmod(item, 4)
        unit = {"y": self.y_units, "x": self.x_units, "z": self.z_units}[link][j]
        slot = 3 * item + {"y": 0, "x": 1, "z": 2}[link]
        ref = self.full(g, unit, self.core, 1 - self.rank)
        return self.copy(ref, ref, self.c_send.at[slot], self.c_recv.at[slot], "c")

    def core_arrival(self, item, link):
        g, j = divmod(item, 4)
        unit = {"y": self.y_units, "x": self.x_units, "z": self.z_units}[link][j]
        slot = 3 * item + {"y": 0, "x": 1, "z": 2}[link]
        ref = self.full(g, unit, 1 - self.core, 1 - self.rank)
        return self.copy(ref, ref, self.c_send.at[slot], self.c_recv.at[slot], "c")

    def y_arrival(self, item):
        g, j = divmod(item, 4)
        ref = self.full(g, self.y_units[j], self.core, 1 - self.rank)
        return self.copy(ref, ref, self.y_send.at[item], self.y_recv.at[item], "y")

    def plane_arrival(self, item, link):
        g, j = divmod(item, 4)
        unit = (self.x_units if link == "x" else self.z_units)[j]
        send, recv = (self.x_send, self.x_recv) if link == "x" else (self.z_send, self.z_recv)
        ref = self.full(g, unit, self.core, 1 - self.rank)
        return self.copy(ref, ref, send.at[item], recv.at[item], link)

    def plan(self):
        lag, hop = self.LAG, self.HOP
        begin = {}
        for item in range(self.count):
            begin["y", item] = item
        for group in range(self.count // 4):
            at = lambda link, j: begin[link, 4 * group + j] + lag
            for link, j in (("x", 0), ("x", 1), ("x", 2), ("z", 0), ("z", 1), ("z", 3)):
                begin[link, 4 * group + j] = at("y", j)
            begin["z", 4 * group + 2] = at("x", 0)
            begin["x", 4 * group + 3] = at("z", 1)
        steps = {}
        order = {"y": 0, "x": 1, "z": 2}
        for (link, item), tick in begin.items():
            arrived = tick + lag
            steps.setdefault(tick, []).append((1, order[link], item, "send", link))
            steps.setdefault(arrived, []).append((0, order[link], item, "arrive", link))
            steps.setdefault(arrived, []).append((2, order[link], item, "share", link))
            steps.setdefault(arrived + hop, []).append((3, order[link], item, "shared", link))
            steps.setdefault(arrived + lag, []).append((4, order[link], item, "sent", link))
        self.steps = {tick: sorted(found) for tick, found in steps.items()}
        self.last_tick = max(steps)
        self.ready = {}
        for tick, found in steps.items():
            for entry in found:
                if entry[3] == "shared":
                    group = entry[2] // 4
                    self.ready[group] = max(self.ready.get(group, 0), tick)

    def tick(self):
        for _, _, item, kind, link in self.steps.get(self.next_tick, []):
            if kind == "send" and link == "y":
                if item % 4 == 0:
                    for load in self.loads[item // 4]:
                        load.wait()
                self.y_copy(item).start()
            elif kind == "send":
                self.plane_copy(item, link).start()
            elif kind == "arrive" and link == "y":
                self.y_arrival(item).wait_recv()
            elif kind == "arrive":
                self.plane_arrival(item, link).wait_recv()
            elif kind == "share":
                self.core_copy(item, link).start()
            elif kind == "shared":
                self.core_arrival(item, link).wait_recv()
            elif link == "y":
                self.y_copy(item).wait_send()
                self.core_copy(item, link).wait_send()
            else:
                self.plane_copy(item, link).wait_send()
                self.core_copy(item, link).wait_send()
        self.next_tick += 1

    def until(self, group):
        while self.next_tick <= self.ready[group]:
            self.tick()

    def finish(self):
        while self.next_tick <= self.last_tick:
            self.tick()


def piece_rows(ref, lead, rows, columns):
    height = rows // 24

    def full(piece, rank):
        start = pl.multiple_of(piece * height, 16)
        left = pl.multiple_of(rank * columns, 128)
        return ref.at[(*lead, pl.ds(start, height), pl.ds(left, columns))]

    return full


def column_groups(ref, lead, rows, columns, parts):
    height, width = rows // 24, columns // parts

    def group(part):
        def full(piece, rank):
            start = pl.multiple_of(piece * height, 16)
            left = pl.multiple_of(rank * columns + part * width, 128)
            return ref.at[(*lead, pl.ds(start, height), pl.ds(left, width))]

        return full

    return [group(part) for part in range(parts)]


def row_groups(ref, lead, rows, parts):
    height = rows // parts // 24

    def group(part):
        def full(piece, rank):
            start = rank * rows + part * (rows // parts) + piece * height
            return ref.at[(*lead, pl.ds(pl.multiple_of(start, 16), height), slice(None))]

        return full

    return [group(part) for part in range(parts)]


def tile_group(ref, rows, columns):
    height, width = rows // 8, columns // 3

    def full(piece, rank):
        start = pl.multiple_of(rank * rows + (piece % 8) * height, 16)
        left = pl.multiple_of((piece // 8) * width, 128)
        return ref.at[pl.ds(start, height), pl.ds(left, width)]

    return full


def gather_kernel(
    wq, wk, wv, wo, wu, wd, mat_a, mat_b,
    dq, bq, dv, bv,
    qkv, out, up, down, full_a, full_b, full_dq, full_bq, full_dv, full_bv,
    load_sem, small_send, small_recv, *sems, stored=(),
):
    levels, model, feat = wq.shape
    hidden, rank_part = wu.shape[2], mat_a.shape[1]
    rank = lax.axis_index("rank")
    parts = 2
    groups, loads = [], []
    used = [0]

    def load(src, dst):
        copy = pltpu.make_async_copy(src, dst, load_sem.at[used[0]])
        used[0] += 1
        copy.start()
        return copy

    def columns_of(size):
        return pl.ds(pl.multiple_of(rank * size, 128), size)

    def rows_of(size):
        return pl.ds(pl.multiple_of(rank * size, 16), size)

    groups.append(piece_rows(full_a, (), model, rank_part))
    loads.append([load(mat_a, full_a.at[:, columns_of(rank_part)])])
    groups.append(tile_group(full_b, rank_part, model))
    loads.append([load(mat_b, full_b.at[rows_of(rank_part), :])])
    for level in range(levels):
        groups.append(piece_rows(qkv, (level, slice(None)), model, feat))
        loads.append([
            load(w.at[level], qkv.at[level, i, :, columns_of(feat)])
            for i, w in enumerate((wq, wk, wv))
        ])
        groups += row_groups(out, (level,), feat, 1)
        loads.append([load(wo.at[level], out.at[level, rows_of(feat), :])])
        groups += column_groups(up, (level,), model, hidden, parts)
        loads.append([load(wu.at[level], up.at[level, :, columns_of(hidden)])])
        loads += [[]] * (parts - 1)
        groups += row_groups(down, (level,), hidden, parts)
        loads.append([load(wd.at[level], down.at[level, rows_of(hidden), :])])
        loads += [[]] * (parts - 1)
    vectors = [(dq, full_dq), (bq, full_bq), (dv, full_dv), (bv, full_bv)]
    small_loads = [load(src, dst.at[:, columns_of(src.shape[1])]) for src, dst in vectors]

    exchange = Exchange(groups, loads, sems)
    exchange.barrier()
    small = []
    for i, (src, dst) in enumerate(vectors):
        ref = dst.at[:, columns_of(src.shape[1])]
        small.append(exchange.copy(src, ref, small_send.at[i], small_recv.at[i], "y"))
        small[-1].start()
    stores = []
    for group, src, dst, sem in stored:
        exchange.until(group)
        stores.append(pltpu.make_async_copy(src, dst, sem))
        stores[-1].start()
    exchange.finish()
    for copy in small:
        copy.wait()
    for copy in stores:
        copy.wait()
    for copy in small_loads:
        copy.wait()


def gather_weights(wq, wk, wv, wo, wu, wd, mat_a, mat_b, dq, bq, dv, bv):
    levels, model, feat = wq.shape
    hidden, rank_part = wu.shape[2], mat_a.shape[1]
    ranks = 2
    low, f32 = jnp.bfloat16, jnp.float32
    shape = jax.ShapeDtypeStruct
    count = 4 * (2 + 6 * levels)
    any_spec = pl.BlockSpec(memory_space=pl.ANY)
    outs = (
        shape((levels, 3, model, ranks * feat), low),
        shape((levels, ranks * feat, model), low),
        shape((levels, model, ranks * hidden), low),
        shape((levels, ranks * hidden, model), low),
        shape((model, ranks * rank_part), low),
        shape((ranks * rank_part, model), low),
        shape((levels, ranks * rank_part), f32),
        shape((levels, ranks * feat), f32),
        shape((levels, ranks * rank_part), f32),
        shape((levels, ranks * feat), f32),
    )
    dma = lambda n: pltpu.SemaphoreType.DMA((n,))
    def kernel(*refs):
        ins, refs = refs[:12], refs[12:]
        outs_hbm, refs = refs[:6], refs[6:]
        vectors, refs = refs[:4], refs[4:]
        vmem, store_sem, refs = refs[:6], refs[6], refs[7:]
        stored = [(0, vmem[4], outs_hbm[4], store_sem.at[0]), (1, vmem[5], outs_hbm[5], store_sem.at[1])]
        for level in range(levels):
            for i, last in enumerate((0, 1, 3, 5)):
                stored.append((2 + 6 * level + last, vmem[i].at[level], outs_hbm[i].at[level],
                               store_sem.at[2 + 4 * level + i]))
        gather_kernel(*ins, *vmem, *vectors, *refs, stored=stored)

    vmem_spec = pl.BlockSpec(memory_space=pltpu.VMEM)
    return pl.pallas_call(
        kernel,
        out_shape=outs,
        in_specs=[any_spec] * 12,
        out_specs=(any_spec,) * 6 + (vmem_spec,) * 4,
        scratch_shapes=[pltpu.VMEM(o.shape, o.dtype) for o in outs[:6]]
        + [dma(2 + 4 * levels), dma(2 + 6 * levels + 4), dma(4), dma(4)]
        + [dma(count) for _ in range(6)]
        + [dma(3 * count)] * 2,
        compiler_params=pltpu.CompilerParams(
            collective_id=0, has_side_effects=True, vmem_limit_bytes=50 * 2**20),
        name="gather_weights",
    )(wq, wk, wv, wo, wu, wd, mat_a, mat_b, dq, bq, dv, bv)


def normalize(values):
    center = values - jnp.mean(values, axis=-1, keepdims=True)
    spread = jnp.mean(center * center, axis=-1, keepdims=True)
    return center * lax.rsqrt(spread + epsilon)


def gelu_exact(values):
    return jax.nn.gelu(values, approximate=False)


def matmul(operand, matrix):
    return jnp.dot(operand, matrix, preferred_element_type=jnp.float32)


def matmul_back(operand, matrix):
    return jnp.einsum("td,ed->te", operand, matrix, preferred_element_type=jnp.float32)


def to_heads(rows, pair_count):
    return rows.reshape(pair_count, -1, rows.shape[1] // HEAD_DIM, HEAD_DIM)


def pair_scores(query_rows, key_rows, key_mask):
    scores = jnp.einsum(
        "qhe,khe->hqk", query_rows, key_rows, preferred_element_type=jnp.float32
    ) * HEAD_DIM ** (-0.5)
    return jnp.where(key_mask[None, None, :], scores, masked)


def attend_pair(pieces):
    query_rows, key_rows, value_rows, key_mask = pieces
    scores = pair_scores(query_rows, key_rows, key_mask)
    row_peak = jnp.max(scores, axis=-1, keepdims=True)
    exponent = jnp.exp(scores - row_peak)
    row_total = jnp.sum(exponent, axis=-1, keepdims=True)
    weights_low = (exponent / row_total).astype(jnp.bfloat16)
    mixed_rows = jnp.einsum(
        "hqk,khe->qhe", weights_low, value_rows, preferred_element_type=jnp.float32
    )
    return (mixed_rows.astype(jnp.bfloat16), row_peak[..., 0] + jnp.log(row_total[..., 0]))


def attend_back(pieces):
    query_rows, key_rows, value_rows, key_mask, log_total, incoming = pieces
    scores = pair_scores(query_rows, key_rows, key_mask)
    probs_full = jnp.exp(scores - log_total[..., None])
    dprob = jnp.einsum("qhe,khe->hqk", incoming, value_rows, preferred_element_type=jnp.float32)
    grad_value = jnp.einsum(
        "hqk,qhe->khe",
        probs_full.astype(jnp.bfloat16),
        incoming,
        preferred_element_type=jnp.float32,
    )
    row_delta = jnp.sum(probs_full * dprob, axis=-1, keepdims=True)
    dscore = (probs_full * (dprob - row_delta)).astype(jnp.bfloat16)
    grad_query = jnp.einsum(
        "hqk,khe->qhe", dscore, key_rows, preferred_element_type=jnp.float32
    ) * HEAD_DIM ** (-0.5)
    grad_key = jnp.einsum(
        "hqk,qhe->khe", dscore, query_rows, preferred_element_type=jnp.float32
    ) * HEAD_DIM ** (-0.5)
    return (
        grad_query.astype(jnp.bfloat16),
        grad_key.astype(jnp.bfloat16),
        grad_value.astype(jnp.bfloat16),
    )


def layer_forward(inputs, key_mask, weights, shared_a, shared_b):
    w_qkv, w_out, w_up, w_down, scale_dq, scale_bq, scale_dv, scale_bv = weights
    rows_low = inputs.astype(jnp.bfloat16)
    inner = matmul(rows_low, shared_a)
    lift_query = matmul((inner * scale_dq).astype(jnp.bfloat16), shared_b)
    lift_value = matmul((inner * scale_dv).astype(jnp.bfloat16), shared_b)
    query_rows = (matmul(rows_low, w_qkv[0]) + lift_query * scale_bq).astype(jnp.bfloat16)
    key_rows = matmul(rows_low, w_qkv[1]).astype(jnp.bfloat16)
    value_rows = (matmul(rows_low, w_qkv[2]) + lift_value * scale_bv).astype(jnp.bfloat16)
    heads = lambda rows: to_heads(rows, 1)[0]
    mixed_rows, log_total = attend_pair(
        (heads(query_rows), heads(key_rows), heads(value_rows), key_mask)
    )
    attended = mixed_rows.reshape(inputs.shape[0], -1)
    first_sum = inputs + matmul(attended, w_out)
    normed = normalize(first_sum)
    before = matmul(normed.astype(jnp.bfloat16), w_up)
    hidden = gelu_exact(before).astype(jnp.bfloat16)
    second_sum = normed + matmul(hidden, w_down)
    saved = (inner, lift_query, lift_value, query_rows, key_rows, value_rows, log_total,
             first_sum, before, second_sum)
    return (normalize(second_sum), saved)


def layer_backward(saved, key_mask, weights, shared_a, shared_b, upstream):
    w_qkv, w_out, w_up, w_down, scale_dq, scale_bq, scale_dv, scale_bv = weights
    (inner, lift_query, lift_value, query_rows, key_rows, value_rows, log_total,
     first_sum, before, second_sum) = saved
    unused, second_back = jax.vjp(normalize, second_sum)
    grad_second = second_back(upstream)[0]
    grad_hidden = matmul_back(grad_second.astype(jnp.bfloat16), w_down)
    unused, gelu_back = jax.vjp(gelu_exact, before)
    grad_before = gelu_back(grad_hidden)[0].astype(jnp.bfloat16)
    unused, first_back = jax.vjp(normalize, first_sum)
    grad_first = first_back(grad_second + matmul_back(grad_before, w_up))[0]
    grad_attended = matmul_back(grad_first.astype(jnp.bfloat16), w_out).astype(jnp.bfloat16)
    heads = lambda rows: to_heads(rows, 1)[0]
    grad_query, grad_key, grad_value = attend_back(
        (heads(query_rows), heads(key_rows), heads(value_rows), key_mask, log_total,
         heads(grad_attended))
    )
    row_count = upstream.shape[0]
    grad_query = grad_query.reshape(row_count, -1)
    grad_key = grad_key.reshape(row_count, -1)
    grad_value = grad_value.reshape(row_count, -1)
    grad_bq = jnp.sum(grad_query.astype(jnp.float32) * lift_query, axis=0)
    grad_bv = jnp.sum(grad_value.astype(jnp.float32) * lift_value, axis=0)
    pass_query = (grad_query * scale_bq).astype(jnp.bfloat16)
    pass_value = (grad_value * scale_bv).astype(jnp.bfloat16)
    rank_query = matmul_back(pass_query, shared_b)
    rank_value = matmul_back(pass_value, shared_b)
    grad_dq = jnp.sum(rank_query * inner, axis=0)
    grad_dv = jnp.sum(rank_value * inner, axis=0)
    grad_inner = (rank_query * scale_dq + rank_value * scale_dv).astype(jnp.bfloat16)
    input_sum = (
        matmul_back(grad_query, w_qkv[0])
        + matmul_back(grad_key, w_qkv[1])
        + matmul_back(grad_value, w_qkv[2])
        + matmul_back(grad_inner, shared_a)
    )
    return (grad_first + input_sum, (grad_dq, grad_bq, grad_dv, grad_bv))


def swap_rows(rows):
    other = lax.ppermute(rows.astype(jnp.bfloat16), "rank", [(0, 1), (1, 0)]).astype(rows.dtype)
    mine_first = lax.axis_index("rank") == 0
    return jnp.concatenate(
        [jnp.where(mine_first, rows, other), jnp.where(mine_first, other, rows)], axis=0
    )


def on_device(tokens, valid_len, w_query, w_key, w_value, w_out, w_up, w_down, mat_a, mat_b,
              scale_dq, scale_bq, scale_dv, scale_bv, cotangent):
    rank = lax.axis_index("rank")
    pair_count = valid_len.shape[0]
    seq_len = tokens.shape[0] // pair_count
    level_count = w_query.shape[0]
    qkv, out, up, down, full_a, full_b, *vectors = gather_weights(
        w_query, w_key, w_value, w_out, w_up, w_down, mat_a, mat_b,
        scale_dq, scale_bq, scale_dv, scale_bv)
    mine = lambda rows: lax.dynamic_slice_in_dim(rows, rank * seq_len, seq_len, 0)
    length = lax.dynamic_index_in_dim(valid_len, rank, 0, keepdims=False)
    key_mask = jnp.arange(seq_len, dtype=jnp.int32) < length
    current = mine(tokens).astype(jnp.float32)
    saved, level_weights = [], []
    for level in range(level_count):
        weights = (qkv[level], out[level], up[level], down[level]) + tuple(v[level] for v in vectors)
        level_weights.append(weights)
        current, kept = layer_forward(current, key_mask, weights, full_a, full_b)
        saved.append(kept)
    upstream = mine(cotangent).astype(jnp.float32)
    collected = [None] * level_count
    for level in reversed(range(level_count)):
        upstream, collected[level] = layer_backward(
            saved[level], key_mask, level_weights[level], full_a, full_b, upstream)
    totals = tuple(jnp.stack([grads[member] for grads in collected]) for member in range(4))
    totals = lax.psum(totals, ("batch", "rank"))
    own = lambda vector: lax.dynamic_slice_in_dim(
        vector, rank * (vector.shape[1] // 2), vector.shape[1] // 2, 1)
    return (swap_rows(current), swap_rows(upstream)) + tuple(own(vector) for vector in totals)


def solution(mesh):
    split = P(None, None, "rank")
    down_split = P(None, "rank", None)
    vector = P(None, "rank")
    return jax.shard_map(
        on_device,
        mesh=mesh,
        in_specs=(P("batch", None), P("batch"), split, split, split, down_split, split, down_split,
                  P(None, "rank"), P("rank", None), vector, vector, vector, vector, P("batch", None)),
        out_specs=(P("batch", None), P("batch", None), vector, vector, vector, vector),
        check_vma=False,
    )
```

time: 1590 us -> 452 us (0.28)
  waiting for transfers between devices: 1010 us -> 19.8 us
  matrix products: 300 us -> 206 us
  Pallas kernels: 0 us -> 79.9 us
  local copies, waits for them, and re-layouts: 112 us -> 48.8 us
  other arithmetic: 81.6 us -> 37.1 us
    psum x8 -> x0, waiting for transfers between devices: 850 us -> none  [the longest x4 478 us: layer_forward(): out_sum = lax.psum(out_part, 'rank')]
    reduce_scatter x4 -> x0, waiting for transfers between devices: 139 us -> none  [the longest x2 71.9 us: layer_forward(): lax.psum_scatter(part_value, 'rank', scatter_dimension=1, tiled=True)]
    pallas_call x0 -> x1, Pallas kernels: none -> 79.9 us  [gather_weights(): pl.pallas_call(kernel, out_shape=outs, in_specs=[any_spec] * 12, out_spec...]
    dot_general x22 -> x18, matrix products: 141 us -> 91.3 us  [matmul(): return jnp.dot(operand, matrix, preferred_element_type=jnp.float32)]
    while x58 -> x0, local copies, waits for them, and re-layouts: 36.6 us -> none  [the longest x10 17.7 us: layer_forward(): lax.map(attend_pair, (to_heads(query_rows, pair_count), to_heads(key_rows...]
    reduce_sum x12 -> x4, other arithmetic: 37.6 us -> 5.97 us  [normalize(): center = values - jnp.mean(values, axis=-1, keepdims=True)]
    dot_general x8 -> x2, matrix products: 29.3 us -> 5.3 us  [attend_pair(): jnp.einsum('hqk,khe->qhe', weights_low, value_rows, preferred_element_typ...]
    sub x4 -> x0, matrix products: 20.4 us -> none  [attend_pair(): exponent = jnp.exp(scores - row_peak)]
  transfers between devices with their start and end apart: 16 -> 2, of which waited for: 14 -> 1; matrix products, arithmetic and copies ran while one was open for 12% -> 1% of each run, Pallas kernels for 0% -> 0%
where the time goes in v1:
time: 452 us; the launch traced here: 447 us
  matrix products  206 us (46%)
  Pallas kernels  79.9 us (18%)
  blocking collectives  52.3 us (12%)
  local copies, waits for them, and re-layouts  48.8 us (11%)
  other arithmetic  37.1 us (8%)
  waiting for transfers between devices  19.8 us (4%)
    dot_general x18, matrix products, matmul(): return jnp.dot(operand, matrix, preferred_element_type=jnp.float32)  91.3 us
    pallas_call x1, Pallas kernels, gather_weights(): pl.pallas_call(kernel, out_shape=outs, in_specs=[any_spec] * 12, out_spec...  79.9 us
    dot_general x18, matrix products, matmul_back(): jnp.einsum('td,ed->te', operand, matrix, preferred_element_type=jnp.float32)  60.5 us
    psum x1, blocking collectives, on_device(): totals = lax.psum(totals, ('batch', 'rank'))  52.3 us
    unnamed x198, local copies, waits for them, and re-layouts  25.6 us
    ppermute x2, waiting for transfers between devices, swap_rows(): lax.ppermute(rows.astype(jnp.bfloat16), 'rank', [(0, 1), (1, 0)])  19.8 us
    dot_general x2, matrix products, attend_back(): jnp.einsum('qhe,khe->hqk', incoming, value_rows, preferred_element_type=j...  17.9 us
    dot_general x2, matrix products, attend_back(): jnp.einsum('hqk,qhe->khe', probs_full.astype(jnp.bfloat16), incoming, pre...  14.7 us
  transfers between devices with their start and end apart: 2, of which 1 were waited for; matrix products, arithmetic and copies ran while one was open for 1% of the time, Pallas kernels for 0%

profile of v1, /device:TPU:0, one launch (start us, length us, event | category | flops | bytes accessed | tf_op | source)
XLA Modules:
  0.0 447.3 jit_solution(1779118862209547146)
XLA Ops:
  2.5 1.3 copy-done
  3.8 1.3 copy-done.1
  10.1 79.9 %gather_weights.1 = (bf16[2,3,768,768]{3,2,1,0:T(8,128)(2,1)}, bf16[2,768,768]{2,1,0:T(8,128)(2,1)}, bf16[2,768,3072]{2,1,0:T(8,128)(2,1)}, bf16[2,3072,768]{2,1...) custom-call(bf16[2,768,384]{2,1,0:T(8,128)(2,1)S(1)} %copy-done, ...), custom_call_target="tpu_custom_call" | custom-call | tf_op jit(solution)/shard_map/gather_weights/pallas_call | solution.py:327
  90.0 2.1 convolution_convert_fusion.3
  92.4 2.9 fusion.147
  97.8 2.9 add_convert_fusion.8
  100.7 1.4 copy.50
  102.2 2.9 fusion.95
  106.3 2.9 add_convert_fusion.9
  109.2 2.3 copy.49
  111.5 3.3 fusion.172
  114.9 1.8 fusion
  116.7 2.7 copy-done.8
  119.4 2.4 fusion.74
  123.1 28.9 %fusion.4 = (f32[512,3072]{1,0:T(8,128)S(1)}, f32[512,3072]{1,0:T(8,128)S(1)}) fusion(bf16[2,768,3072]{2,1,0:T(8,128)(2,1)} %get-tuple-element.24, f32[512,768]{1,0:T(8,128)S(1)} %get-tuple-element.63, f32[512]{0:T(512)S(1)} %fusion.150, f32[512]{0:T(512)S(1)} %broadcast_multiply_fusion.3), kind=kOutput, calls=%fused_computation.18 | convolution fusion | flops 2514616320 | bytes 18878464 | tf_op jit(solution)/shard_map/dot_general | solution.py:353
  152.1 2.8 fusion.174
  154.9 1.7 copy-done.20
  157.1 3.3 convolution_convert_fusion.2
  160.4 2.3 fusion.179
  162.7 2.3 copy.55
  165.0 2.6 fusion.98
  168.8 3.0 add_convert_fusion.6
  171.8 2.4 copy.54
  174.2 2.6 fusion.97
  178.0 3.0 add_convert_fusion.7
  181.0 2.3 copy.53
  183.3 4.1 fusion.175
  187.4 1.8 fusion.1
  189.2 2.8 copy-done.9
  192.0 2.9 fusion.73
  196.1 17.6 %fusion.5 = (f32[512,3072]{1,0:T(8,128)S(1)}, f32[512,3072]{1,0:T(8,128)S(1)}) fusion(bf16[2,768,3072]{2,1,0:T(8,128)(2,1)} %get-tuple-element.24, f32[512,768]{1,0:T(8,128)S(1)} %get-tuple-element.71, f32[512]{0:T(512)S(1)} %fusion.152, f32[512]{0:T(512)S(1)} %broadcast_multiply_fusion.1), kind=kOutput, calls=%fused_computation.19 | convolution fusion | flops 2514616320 | bytes 18878464 | tf_op jit(solution)/shard_map/dot_general | solution.py:353
  213.8 8.7 %fusion.177 = (f32[512]{0:T(512)S(1)}, f32[512,768]{1,0:T(8,128)S(1)}) fusion(bf16[2,3072,768]{2,1,0:T(8,128)(2,1)} %get-tuple-element.25, f32[512,3072]{1,0:T(8,128)S(1)} %get-tuple-element.72, f32[512,3072]{1,0:T(8,128)S(1)} %get-tuple-element.73, f32[512]{0:T(512)S(1)} %fusion.152, f32[512,768]{1,0:T(8,128)S(1)} %get-tuple-element.71, ...), kind=kOutput, calls=%fused_computation.289 | convolution fusion | flops 2422210048 | bytes 20453376 | tf_op jit(solution)/shard_map/dot_general | solution.py:353
  224.9 19.8 %collective-permute-done = bf16[512,768]{1,0:T(8,128)(2,1)} collective-permute-done((bf16[512,768]{1,0:T(8,128)(2,1)}, bf16[512,768]{1,0:T(8,128)(2,1)}, u32[]{:S(2)}, u32[]{:S(2)}) %collective-permute-start) | collective-permute-done | bytes 786464 | tf_op jit(solution)/shard_map/ppermute | solution.py:474
  244.7 4.4 fusion.169
  249.1 7.2 %fusion.24 = f32[512,3072]{1,0:T(8,128)} fusion(bf16[2,3072,768]{2,1,0:T(8,128)(2,1)} %get-tuple-element.25, f32[512,768]{1,0:T(8,128)S(1)} %get-tuple-element.47, f32[512]{0:T(512)S(1)} %negate_multiply_fusion.5), kind=kOutput, calls=%fused_computation.56 | convolution fusion | flops 2416705536 | bytes 12584960 | tf_op jit(solution)/shard_map/td,ed->te/dot_general | solution.py:357
  256.3 9.1 %multiply_reduce_fusion.8 = (f32[512]{0:T(512)S(1)}, f32[512,768]{1,0:T(8,128)S(1)}) fusion(f32[512,768]{1,0:T(8,128)S(1)} %copy-done.15, f32[512]{0:T(512)S(1)} %broadcast_multiply_fusion.1, bf16[2,768,3072]{2,1,0:T(8,128)(2,1)} %get-tuple-element.24, f32[512,3072]{1,0:T(8,128)} %fusion.24, f32[512,3072]{1,0:T(8,128)S(1)} %bitcast.180, ...), kind=kOutput, calls=%fused_computation.129 | convolution fusion | flops 2439904768 | bytes 28317696 | tf_op jit(solution)/shard_map/td,ed->te/dot_general | solution.py:357
  267.5 1.7 convolution_convert_fusion.1
  269.2 2.3 copy.57
  271.5 7.9 %fusion.67 = bf16[12,64,512]{2,1,0:T(8,128)(2,1)} fusion(bf16[512,12,64]{0,2,1:T(8,128)(2,1)} %bitcast.189, f32[12,512,512]{1,2,0:T(8,128)} %copy-done.9, f32[12,512]{1,0:T(8,128)S(1)} %log_add_fusion.1), kind=kOutput, calls=%fused_computation.155 | convolution fusion | flops 409337856 | bytes 14180352 | tf_op jit(solution)/shard_map/hqk,qhe->khe/dot_general | solution.py:389
  279.4 9.0 %multiply_reduce_fusion.1 = (f32[12,512]{1,0:T(8,128)S(1)}, f32[12,512,512]{1,2,0:T(8,128)}) fusion(f32[12,512,512]{1,2,0:T(8,128)} %copy-done.9, f32[12,512]{1,0:T(8,128)S(1)} %log_add_fusion.1, bf16[512,12,64]{0,2,1:T(8,128)(2,1)S(1)} %bitcast.190, bf16[512,12,64]{0,2,1:T(8,128)(2,1)S(1)} %bitcast.208), kind=kOutput, calls=%fused_computation.4 | convolution fusion | flops 412084224 | bytes 26787840 | tf_op jit(solution)/shard_map/qhe,khe->hqk/dot_general | solution.py:388
  288.4 7.3 %multiply_convert_fusion.1 = bf16[12,512,512]{1,2,0:T(8,128)(2,1)S(1)} fusion(f32[12,512,512]{1,2,0:T(8,128)} %get-tuple-element.79, f32[12,512,512]{1,2,0:T(8,128)S(1)} %bitcast.176, f32[12,512]{1,0:T(8,128)S(1)} %get-tuple-element.78, f32[12,512]{1,0:T(8,128)S(1)} %log_add_fusion.1), kind=kLoop, calls=%fused_computation.3 | loop fusion | flops 12582912 | bytes 31506432 | tf_op jit(solution)/shard_map/convert_element_type | solution.py:396
  295.8 2.9 multiply_convert_fusion.12
  298.7 2.0 multiply_convert_fusion.13
  300.7 2.3 copy.61
  303.0 3.6 fusion.80
  306.9 2.3 fusion.131
  309.3 2.3 copy.62
  311.6 1.9 fusion.54
  313.5 2.5 fusion.77
  319.7 3.1 multiply_reduce_fusion.7
  323.5 4.7 %fusion.32 = f32[512,3072]{1,0:T(8,128)} fusion(bf16[2,3072,768]{2,1,0:T(8,128)(2,1)S(1)} %bitcast.188, f32[512,768]{1,0:T(8,128)S(1)} %get-tuple-element.43, f32[512]{0:T(512)S(1)} %negate_multiply_fusion.3), kind=kOutput, calls=%fused_computation.64 | convolution fusion | flops 2416705536 | bytes 12584960 | tf_op jit(solution)/shard_map/td,ed->te/dot_general | solution.py:357
  328.2 9.3 %multiply_reduce_fusion.6 = (f32[512]{0:T(512)S(1)}, f32[512,768]{1,0:T(8,128)S(1)}) fusion(f32[512,768]{1,0:T(8,128)S(1)} %copy-done.13, f32[512]{0:T(512)S(1)} %copy-done.62, bf16[2,768,3072]{2,1,0:T(8,128)(2,1)} %get-tuple-element.24, f32[512,3072]{1,0:T(8,128)} %fusion.32, f32[512,3072]{1,0:T(8,128)S(1)} %bitcast.178, f32[512,3072]{1,0:T(8,128)} %copy-done.20, ...), kind=kOutput, calls=%fused_computation.124 | convolution fusion | flops 2439904768 | bytes 28317696 | tf_op jit(solution)/shard_map/td,ed->te/dot_general | solution.py:357
  340.8 6.8 %fusion.70 = bf16[12,64,512]{2,1,0:T(8,128)(2,1)S(1)} fusion(bf16[512,12,64]{0,2,1:T(8,128)(2,1)S(1)} %bitcast.191, f32[12,512,512]{1,2,0:T(8,128)} %copy-done.8, f32[12,512]{1,0:T(8,128)S(1)} %log_add_fusion), kind=kOutput, calls=%fused_computation.156 | convolution fusion | flops 409337856 | bytes 14180352 | tf_op jit(solution)/shard_map/hqk,qhe->khe/dot_general | solution.py:389
  347.6 8.9 %multiply_reduce_fusion = (f32[12,512]{1,0:T(8,128)S(1)}, f32[12,512,512]{1,2,0:T(8,128)}) fusion(f32[12,512,512]{1,2,0:T(8,128)} %copy-done.8, f32[12,512]{1,0:T(8,128)S(1)} %log_add_fusion, bf16[512,12,64]{0,2,1:T(8,128)(2,1)S(1)} %bitcast.192, bf16[512,12,64]{0,2,1:T(8,128)(2,1)S(1)} %bitcast.206), kind=kOutput, calls=%fused_computation.1 | convolution fusion | flops 412084224 | bytes 26787840 | tf_op jit(solution)/shard_map/qhe,khe->hqk/dot_general | solution.py:388
  356.6 6.9 %multiply_convert_fusion = bf16[12,512,512]{1,2,0:T(8,128)(2,1)S(1)} fusion(f32[12,512,512]{1,2,0:T(8,128)} %get-tuple-element.85, f32[12,512,512]{1,2,0:T(8,128)S(1)} %bitcast.174, f32[12,512]{1,0:T(8,128)S(1)} %get-tuple-element.84, f32[12,512]{1,0:T(8,128)S(1)} %log_add_fusion), kind=kLoop, calls=%fused_computation | loop fusion | flops 12582912 | bytes 31506432 | tf_op jit(solution)/shard_map/convert_element_type | solution.py:396
  363.5 2.9 multiply_convert_fusion.10
  368.7 3.4 fusion.90
  372.3 2.3 fusion.127
  375.0 1.8 fusion.58
  376.7 2.5 fusion.87
  382.6 3.7 fusion.178
  387.0 52.3 %all-reduce = (f32[2,1024]{1,0:T(2,128)S(1)}, f32[2,768]{1,0:T(2,128)S(1)}, f32[2,1024]{1,0:T(2,128)S(1)}, f32[2,768]{1,0:T(2,128)S(1)}) all-reduce(f32[2,1024]{1,0:T(2,128)S(1)} %pad_maximum_fusion.2, f32[2,768]{1,0:T(2,128)S(1)} %pad_maximum_fusion.4, ...), channel_id=1, replica_groups=mesh['batch'=16,'rank'=2] {'batch','rank'}, use_global_device_ids=true, to_apply=%region_24.25 | all-reduce | flops 7168 | bytes 57344 | tf_op jit(solution)/shard_map/psum | solution.py:506
  441.6 3.4 pad_maximum_fusion
  445.3 1.9 pad_maximum_fusion.1
  (260 shorter events, 37.9 us)
Async XLA Ops:
  10.1 79.9 %copy-start.79 = (bf16[1024,768]{1,0:T(8,128)(2,1)S(1)}, bf16[1024,768]{1,0:T(8,128)(2,1)}, u32[]{:S(2)}) copy-start(bf16[1024,768]{1,0:T(8,128)(2,1)} %param.15) | copy-start | bytes 4718596
  92.3 19.2 %copy-start.23 = (bf16[512,768]{0,1:T(8,128)(2,1)}, bf16[512,768]{0,1:T(8,128)(2,1)S(1)}, u32[]{:S(2)}) copy-start(bf16[512,768]{0,1:T(8,128)(2,1)S(1)} %copy.51) | copy-start | bytes 2359300
  92.4 3.1 copy-start.10
  95.4 6.8 %copy-start.67 = (f32[1,1024]{1,0:T(1,128)}, f32[1,1024]{1,0:T(1,128)S(1)}, u32[]{:S(2)}) copy-start(f32[1,1024]{1,0:T(1,128)S(1)} %get-tuple-element.92) | copy-start | bytes 12292
  95.4 9.7 %copy-start.71 = (f32[768]{0:T(1024)}, f32[768]{0:T(1024)S(1)}, u32[]{:S(2)}) copy-start(f32[768]{0:T(1024)S(1)} %get-tuple-element.90) | copy-start | bytes 9220
  102.2 9.4 %copy-start.31 = (bf16[512,768]{0,1:T(8,128)(2,1)}, bf16[512,768]{0,1:T(8,128)(2,1)S(1)}, u32[]{:S(2)}) copy-start(bf16[512,768]{0,1:T(8,128)(2,1)S(1)} %copy.50) | copy-start | bytes 2359300
  102.2 4.1 copy-start.81
  114.8 4.5 %copy-start.8 = (f32[12,512,512]{1,2,0:T(8,128)}, f32[12,512,512]{1,2,0:T(8,128)S(1)}, u32[]{:S(2)}) copy-start(f32[12,512,512]{1,2,0:T(8,128)S(1)} %get-tuple-element.61) | copy-start | bytes 37748740
  114.9 4.5 %copy-start.49 = (bf16[512,768]{0,1:T(8,128)(2,1)S(1)}, bf16[512,768]{0,1:T(8,128)(2,1)}, u32[]{:S(2)}) copy-start(bf16[512,768]{0,1:T(8,128)(2,1)} %copy.49) | copy-start | bytes 2359300
  121.8 30.2 %slice-start.10 = ((s8[9437184]{0:T(1024)(128)(4,1)}), s8[4194304]{0:T(1024)(128)(4,1)S(1)}, s32[]{:S(2)}) async-start(s8[9437184]{0:T(1024)(128)(4,1)} %bitcast.185), calls=%async_computation.10 | async-start | bytes 8388608
  122.8 29.3 %copy-start.12 = (f32[512,768]{1,0:T(8,128)}, f32[512,768]{1,0:T(8,128)S(1)}, u32[]{:S(2)}) copy-start(f32[512,768]{1,0:T(8,128)S(1)} %get-tuple-element.63) | copy-start | bytes 4718596
  122.8 29.3 %copy-start.61 = (f32[512]{0:T(512)}, f32[512]{0:T(512)S(1)}, u32[]{:S(2)}) copy-start(f32[512]{0:T(512)S(1)} %broadcast_multiply_fusion.3) | copy-start | bytes 6148
  123.1 28.9 %copy-start.69 = (f32[512]{0:T(512)}, f32[512]{0:T(512)S(1)}, u32[]{:S(2)}) copy-start(f32[512]{0:T(512)S(1)} %multiply_reduce_fusion.12) | copy-start | bytes 6148
  123.1 28.9 %copy-start.63 = (f32[512]{0:T(512)}, f32[512]{0:T(512)S(1)}, u32[]{:S(2)}) copy-start(f32[512]{0:T(512)S(1)} %fusion.150) | copy-start | bytes 6148
  123.1 29.0 %slice-start.11 = ((s8[9437184]{0:T(1024)(128)(4,1)}), s8[4194304]{0:T(1024)(128)(4,1)S(1)}, s32[]{:S(2)}) async-start(s8[9437184]{0:T(1024)(128)(4,1)} %bitcast.185), calls=%async_computation.11 | async-start | bytes 8388608
  123.1 29.0 %slice-start.12 = ((s8[9437184]{0:T(1024)(128)(4,1)}), s8[1048576]{0:T(1024)(128)(4,1)S(1)}, s32[]{:S(2)}) async-start(s8[9437184]{0:T(1024)(128)(4,1)} %bitcast.185), calls=%async_computation.12 | async-start | bytes 2097152
  152.0 2.9 copy-start.19
  152.0 4.5 %copy-start.20 = (f32[512,3072]{1,0:T(8,128)}, f32[512,3072]{1,0:T(8,128)S(1)}, u32[]{:S(2)}) copy-start(f32[512,3072]{1,0:T(8,128)S(1)} %get-tuple-element.65) | copy-start | bytes 18874372
  157.1 3.3 copy-start.58
  157.1 3.3 copy-start.41
  165.0 3.9 copy-start.59
  174.2 3.9 copy-start.60
  187.4 4.6 %copy-start.9 = (f32[12,512,512]{1,2,0:T(8,128)}, f32[12,512,512]{1,2,0:T(8,128)S(1)}, u32[]{:S(2)}) copy-start(f32[12,512,512]{1,2,0:T(8,128)S(1)} %get-tuple-element.69) | copy-start | bytes 37748740
  187.4 4.6 %copy-start.51 = (bf16[512,768]{0,1:T(8,128)(2,1)S(1)}, bf16[512,768]{0,1:T(8,128)(2,1)}, u32[]{:S(2)}) copy-start(bf16[512,768]{0,1:T(8,128)(2,1)} %copy.53) | copy-start | bytes 2359300
  195.8 18.0 %copy-start.14 = (f32[512,768]{1,0:T(8,128)}, f32[512,768]{1,0:T(8,128)S(1)}, u32[]{:S(2)}) copy-start(f32[512,768]{1,0:T(8,128)S(1)} %get-tuple-element.71) | copy-start | bytes 4718596
  213.7 8.7 %copy-start.21 = (f32[512,3072]{1,0:T(8,128)}, f32[512,3072]{1,0:T(8,128)S(1)}, u32[]{:S(2)}) copy-start(f32[512,3072]{1,0:T(8,128)S(1)} %get-tuple-element.72) | copy-start | bytes 18874372
  213.8 8.7 %copy-start.22 = (f32[512,3072]{1,0:T(8,128)}, f32[512,3072]{1,0:T(8,128)S(1)}, u32[]{:S(2)}) copy-start(f32[512,3072]{1,0:T(8,128)S(1)} %get-tuple-element.73) | copy-start | bytes 18874372
  213.8 8.7 %copy-start.55 = (bf16[1024,768]{1,0:T(8,128)(2,1)S(1)}, bf16[1024,768]{1,0:T(8,128)(2,1)}, u32[]{:S(2)}) copy-start(bf16[1024,768]{1,0:T(8,128)(2,1)} %param.29) | copy-start | bytes 4718596
  224.2 20.5 %collective-permute-start = (bf16[512,768]{1,0:T(8,128)(2,1)}, bf16[512,768]{1,0:T(8,128)(2,1)}, u32[]{:S(2)}, u32[]{:S(2)}) collective-permute-start(bf16[512,768]{1,0:T(8,128)(2,1)} %multiply_convert_fusion.21), channel_id=1, source_target_pairs={{0,1},{1,0},{2,3},{3,2},{4,5},{5,4},{6,7},{7,6},{8,9},{9,8},{10,11... | collective-permute-start | bytes 2359304 | tf_op jit(solution)/shard_map/ppermute | solution.py:474
  244.7 11.6 %slice-start.8 = ((s8[6291456]{0:T(1024)(128)(4,1)}), s8[4194304]{0:T(1024)(128)(4,1)S(1)}, s32[]{:S(2)}) async-start(s8[6291456]{0:T(1024)(128)(4,1)} %bitcast.179), calls=%async_computation.8 | async-start | bytes 8388608
  249.1 7.2 %copy-start.15 = (f32[512,768]{1,0:T(8,128)S(1)}, f32[512,768]{1,0:T(8,128)}, u32[]{:S(2)}) copy-start(f32[512,768]{1,0:T(8,128)} %copy-done.14) | copy-start | bytes 4718596
  249.1 7.2 %slice-start.9 = ((s8[6291456]{0:T(1024)(128)(4,1)}), s8[2097152]{0:T(1024)(128)(4,1)S(1)}, s32[]{:S(2)}) async-start(s8[6291456]{0:T(1024)(128)(4,1)} %bitcast.179), calls=%async_computation.9 | async-start | bytes 4194304
  271.5 7.9 %copy-start.28 = (bf16[512,768]{0,1:T(8,128)(2,1)S(1)}, bf16[512,768]{0,1:T(8,128)(2,1)}, u32[]{:S(2)}) copy-start(bf16[512,768]{0,1:T(8,128)(2,1)} %copy.57) | copy-start | bytes 2359300
  271.5 7.9 %copy-start.52 = (bf16[512,768]{0,1:T(8,128)(2,1)S(1)}, bf16[512,768]{0,1:T(8,128)(2,1)}, u32[]{:S(2)}) copy-start(bf16[512,768]{0,1:T(8,128)(2,1)} %copy.53) | copy-start | bytes 2359300
  271.5 16.9 %slice-start.3 = ((s8[12582912]{0:T(1024)(128)(4,1)}), s8[4194304]{0:T(1024)(128)(4,1)S(1)}, s32[]{:S(2)}) async-start(s8[12582912]{0:T(1024)(128)(4,1)} %bitcast.175), calls=%async_computation.3 | async-start | bytes 8388608
  271.5 16.9 %slice-start.4 = ((s8[12582912]{0:T(1024)(128)(4,1)}), s8[4194304]{0:T(1024)(128)(4,1)S(1)}, s32[]{:S(2)}) async-start(s8[12582912]{0:T(1024)(128)(4,1)} %bitcast.175), calls=%async_computation.4 | async-start | bytes 8388608
  279.4 9.0 %slice-start.5 = ((s8[12582912]{0:T(1024)(128)(4,1)}), s8[4194304]{0:T(1024)(128)(4,1)S(1)}, s32[]{:S(2)}) async-start(s8[12582912]{0:T(1024)(128)(4,1)} %bitcast.175), calls=%async_computation.5 | async-start | bytes 8388608
  288.4 7.3 %copy-start.33 = (bf16[512,768]{0,1:T(8,128)(2,1)S(1)}, bf16[512,768]{0,1:T(8,128)(2,1)}, u32[]{:S(2)}) copy-start(bf16[512,768]{0,1:T(8,128)(2,1)} %copy.54) | copy-start | bytes 2359300
  295.8 2.9 copy-start.25
  303.0 3.6 copy-start.40
  303.0 3.6 copy-start.53
  311.6 4.5 copy-start.27
  316.1 7.3 %slice-start.13 = ((s8[9437184]{0:T(1024)(128)(4,1)}), s8[4194304]{0:T(1024)(128)(4,1)S(1)}, s32[]{:S(2)}) async-start(s8[9437184]{0:T(1024)(128)(4,1)} %bitcast.187), calls=%async_computation.13 | async-start | bytes 8388608
  317.5 6.0 %slice-start.14 = ((s8[9437184]{0:T(1024)(128)(4,1)}), s8[4194304]{0:T(1024)(128)(4,1)S(1)}, s32[]{:S(2)}) async-start(s8[9437184]{0:T(1024)(128)(4,1)} %bitcast.187), calls=%async_computation.14 | async-start | bytes 8388608
  319.7 3.7 slice-start.15
  319.7 8.5 %slice-start.6 = ((s8[6291456]{0:T(1024)(128)(4,1)}), s8[4194304]{0:T(1024)(128)(4,1)S(1)}, s32[]{:S(2)}) async-start(s8[6291456]{0:T(1024)(128)(4,1)} %bitcast.177), calls=%async_computation.6 | async-start | bytes 8388608
  322.9 5.3 %slice-start.7 = ((s8[6291456]{0:T(1024)(128)(4,1)}), s8[2097152]{0:T(1024)(128)(4,1)S(1)}, s32[]{:S(2)}) async-start(s8[6291456]{0:T(1024)(128)(4,1)} %bitcast.177), calls=%async_computation.7 | async-start | bytes 4194304
  323.5 4.7 %copy-start.13 = (f32[512,768]{1,0:T(8,128)S(1)}, f32[512,768]{1,0:T(8,128)}, u32[]{:S(2)}) copy-start(f32[512,768]{1,0:T(8,128)} %copy-done.12) | copy-start | bytes 4718596
  323.5 4.7 %copy-start.62 = (f32[512]{0:T(512)S(1)}, f32[512]{0:T(512)}, u32[]{:S(2)}) copy-start(f32[512]{0:T(512)} %copy-done.61) | copy-start | bytes 6148
  328.2 9.3 %copy-start.70 = (f32[512]{0:T(512)S(1)}, f32[512]{0:T(512)}, u32[]{:S(2)}) copy-start(f32[512]{0:T(512)} %copy-done.69) | copy-start | bytes 6148
  328.2 9.3 %copy-start.64 = (f32[512]{0:T(512)S(1)}, f32[512]{0:T(512)}, u32[]{:S(2)}) copy-start(f32[512]{0:T(512)} %copy-done.63) | copy-start | bytes 6148
  340.8 6.8 %copy-start.50 = (bf16[512,768]{0,1:T(8,128)(2,1)S(1)}, bf16[512,768]{0,1:T(8,128)(2,1)}, u32[]{:S(2)}) copy-start(bf16[512,768]{0,1:T(8,128)(2,1)} %copy.49) | copy-start | bytes 2359300
  340.8 15.8 %slice-start = ((s8[12582912]{0:T(1024)(128)(4,1)}), s8[4194304]{0:T(1024)(128)(4,1)S(1)}, s32[]{:S(2)}) async-start(s8[12582912]{0:T(1024)(128)(4,1)} %bitcast.173), calls=%async_computation | async-start | bytes 8388608
  340.8 15.7 %slice-start.1 = ((s8[12582912]{0:T(1024)(128)(4,1)}), s8[4194304]{0:T(1024)(128)(4,1)S(1)}, s32[]{:S(2)}) async-start(s8[12582912]{0:T(1024)(128)(4,1)} %bitcast.173), calls=%async_computation.1 | async-start | bytes 8388608
  347.6 9.0 %slice-start.2 = ((s8[12582912]{0:T(1024)(128)(4,1)}), s8[4194304]{0:T(1024)(128)(4,1)S(1)}, s32[]{:S(2)}) async-start(s8[12582912]{0:T(1024)(128)(4,1)} %bitcast.173), calls=%async_computation.2 | async-start | bytes 8388608
  356.5 6.9 %copy-start.32 = (bf16[512,768]{0,1:T(8,128)(2,1)S(1)}, bf16[512,768]{0,1:T(8,128)(2,1)}, u32[]{:S(2)}) copy-start(bf16[512,768]{0,1:T(8,128)(2,1)} %copy-done.31) | copy-start | bytes 2359300
  363.5 2.9 copy-start.24
  368.7 3.4 copy-start.37
  368.7 3.4 copy-start.54
  368.7 3.6 copy-start.74
  374.9 4.3 copy-start.26
  382.6 59.1 %copy-start.34 = (f32[512,768]{1,0:T(8,128)S(1)}, f32[512,768]{1,0:T(8,128)}, u32[]{:S(2)}) copy-start(f32[512,768]{1,0:T(8,128)} %get-tuple-element.52) | copy-start | bytes 4718596
  386.3 58.8 %collective-permute-start.1 = (bf16[512,768]{1,0:T(8,128)(2,1)S(1)}, bf16[512,768]{1,0:T(8,128)(2,1)S(1)}, u32[]{:S(2)}, u32[]{:S(2)}) collective-permute-start(bf16[512,768]{1,0:T(8,128)(2,1)S(1)} %get-tuple-element.86), channel_id=1, source_target_pairs={{0,1},{1,0},{2,3},{3,2},{4,5},{5,4},{6,7},{7,6},{8,9},{9,8},{10,11... | collective-permute-start | bytes 2359304 | tf_op jit(solution)/shard_map/ppermute | solution.py:474
  441.6 3.4 copy-start.46
  (37 other events, 60.2 us)
